TPU v7x, 32 devices: a whole 2x2x4 slice. The times are simulated.
32 devices in a mesh: row: 8 (over y, x, core), col: 4 (over z).
Axes of the slice: x: 2, y: 2, z: 4, core: 2. Of those that a mesh axis runs over, the one named last changes fastest.
Arguments:
- diag_tiles: float32 [32, 256, 256], P('row'), as said below
- left_fac: bfloat16 [32, 32, 256, 128], P('row', 'col'), as said below
- right_fac: bfloat16 [32, 32, 256, 128], P('row', 'col'), as said below
- ranks: int32 [32, 32], replicated, may hold values from 16 to 128, as said below
Outputs:
- factored: float32 [32, 32, 256, 256], P('row', 'col')
Inputs may be any that keep to these rules, and one draw needn't show every extreme that they name: `ranks`: every entry is a multiple of 16; in every draw some tile below the diagonal has rank 128, and the mean rank is about a third of 128. `diag_tiles`: every tile is symmetric; the first diagonal tile and the updated second diagonal tile M are positive definite. `left_fac`: entries have mean zero and deviation one. `right_fac`: entries have mean zero and deviation one over the square root of 128.
All inputs are finite; a program needn't handle non-finite values.
Results may differ from a plain program's by a relative error of at most 0.0003.
Values sent between devices are 32-bit elements; how exact they have to be, the bound alone decides.
No kernel may reach another device: no remote copies, remote signals or barrier semaphores. Data moves between devices by JAX's collectives and lax.ppermute only.
A program may use at most 64 MiB of HBM per device.

v0:
```python
import jax
import jax.numpy as jnp
from jax import lax
from jax.sharding import PartitionSpec as P

PRECISE = lax.Precision.HIGHEST


def from_root(shard, axis, root):
    mine = lax.axis_index(axis) == root
    return lax.psum(jnp.where(mine, shard, jnp.zeros_like(shard)), axis)


def lower_solve(factor, stacked):
    pieces, tile_width, rank_cap = stacked.shape
    flattened = jnp.transpose(stacked, (1, 0, 2)).reshape(tile_width, pieces * rank_cap)
    solved = lax.linalg.triangular_solve(factor, flattened, left_side=True, lower=True)
    return jnp.transpose(solved.reshape(tile_width, pieces, rank_cap), (1, 0, 2))


def expand(left_basis, weights):
    return jnp.einsum("nbr,ncr->nbc", left_basis, weights, precision=PRECISE)


def correction(head_basis, row_solved, pivot_solved):
    mixing = jnp.einsum("nbr,bs->nrs", row_solved, pivot_solved, precision=PRECISE)
    return -jnp.einsum("bs,nrs->nbr", head_basis, mixing, precision=PRECISE)


def take_slot(stacked, holder_slot):
    return lax.dynamic_index_in_dim(stacked, holder_slot, 0, keepdims=False)


def shards(diag_tiles, left_fac, right_fac, ranks):
    grid_rows = lax.axis_size("row")
    grid_cols = lax.axis_size("col")
    row_here = lax.axis_index("row")
    col_here = lax.axis_index("col")
    row_slots, col_slots, tile_width, rank_cap = left_fac.shape
    tile_rows = jnp.arange(row_slots, dtype=jnp.int32) * grid_rows + row_here
    tile_cols = jnp.arange(col_slots, dtype=jnp.int32) * grid_cols + col_here
    local_ranks = jnp.take(jnp.take(ranks, tile_rows, axis=0), tile_cols, axis=1)
    columns_live = jnp.arange(rank_cap, dtype=jnp.int32)[None, None, :] < local_ranks[:, :, None]
    left_bases = jnp.where(columns_live[:, :, None, :], left_fac.astype(jnp.float32), 0.0)
    right_coefs = right_fac.astype(jnp.float32)
    first_pivot = from_root(jnp.linalg.cholesky(diag_tiles[0]), "row", 0)
    first_local = lower_solve(first_pivot, right_coefs[:, 0])
    first_row_basis, first_row_solved = (
        from_root(left_bases[:, 0], "col", 0),
        from_root(first_local, "col", 0),
    )
    gathered_basis = []
    gathered_solved = []
    for column_slot in range(col_slots):
        tile_number = column_slot * grid_cols + col_here
        holder_slot = tile_number // grid_rows
        received = (
            from_root(take_slot(first_row_basis, holder_slot), "row", tile_number % grid_rows),
            from_root(take_slot(first_row_solved, holder_slot), "row", tile_number % grid_rows),
        )
        gathered_basis.append(received[0])
        gathered_solved.append(received[1])
    first_col_basis = jnp.stack(gathered_basis)
    first_col_solved = jnp.stack(gathered_solved)
    pivot_basis = first_row_basis[0]
    pivot_solved = first_row_solved[0]
    pivot_cross = jnp.einsum("br,bs->rs", pivot_solved, pivot_solved, precision=PRECISE)
    partial_term = jnp.matmul(pivot_basis, pivot_cross, precision=PRECISE)
    shifted = diag_tiles[0] - jnp.matmul(partial_term, pivot_basis.T, precision=PRECISE)
    second_pivot = from_root(jnp.linalg.cholesky(shifted), "row", 1)
    second_local = lower_solve(second_pivot, right_coefs[:, 0])
    first_row_dense = expand(first_row_basis, first_row_solved)
    first_col_dense = expand(first_col_basis, first_col_solved)
    pieces_dense = []
    local_head = lax.linalg.triangular_solve(
        second_pivot, first_col_basis[0], left_side=True, lower=True
    )
    local_minus = correction(local_head, first_row_solved, first_col_solved[0])
    second_row = (
        from_root(left_bases[:, 0], "col", 1),
        from_root(second_local, "col", 1),
        from_root(local_minus, "col", 1),
    )
    second_row_dense = expand(second_row[0], second_row[1]) + expand(first_row_basis, second_row[2])
    for column_slot in range(col_slots):
        tile_number = column_slot * grid_cols + col_here
        holder_slot = tile_number // grid_rows
        received = (
            from_root(take_slot(second_row[0], holder_slot), "row", tile_number % grid_rows),
            from_root(take_slot(second_row[1], holder_slot), "row", tile_number % grid_rows),
            from_root(take_slot(second_row[2], holder_slot), "row", tile_number % grid_rows),
        )
        own_dense = expand(received[0][None], received[1][None]) + expand(
            first_col_basis[column_slot][None], received[2][None]
        )
        pieces_dense.append(own_dense[0])
    second_col_dense = jnp.stack(pieces_dense)
    dense_front = jnp.einsum("lmbr,lmcr->lmbc", left_bases, right_coefs, precision=PRECISE)
    updates = jnp.einsum("lbk,mck->lmbc", first_row_dense, first_col_dense, precision=PRECISE)
    updates = updates + jnp.einsum(
        "lbk,mck->lmbc", second_row_dense, second_col_dense, precision=PRECISE
    )
    schur = dense_front - updates
    row_ids = tile_rows[:, None, None, None]
    col_ids = tile_cols[None, :, None, None]
    chosen = jnp.where(
        col_ids == 0,
        first_row_dense[:, None],
        jnp.where(col_ids == 1, second_row_dense[:, None], schur),
    )
    return jnp.where(col_ids < row_ids, chosen, 0.0)


def solution(mesh):
    in_specs = (P("row", None, None), P("row", "col", None, None), P("row", "col", None, None), P())
    out_specs = P("row", "col", None, None)
    return jax.shard_map(shards, mesh=mesh, in_specs=in_specs, out_specs=out_specs, check_vma=False)
```

profile of v0, /device:TPU:21, one launch (start us, length us, event | category | flops | bytes accessed | tf_op | source)
XLA Modules:
  0.0 545.9 jit_solution(4549453439229039747)
XLA Ops:
  6.5 1.0 slice.68
  7.7 1.1 fusion.33
  8.9 11.7 %cholesky.130 = f32[128,128]{1,0:T(8,128)S(1)} custom-call(f32[128,128]{1,0:T(8,128)S(1)} %cholesky.194), custom_call_target="Cholesky" | custom-call | tf_op jit(solution)/shard_map/jit(cholesky)/cholesky | solution.py:46
  20.6 9.8 %custom-call.17 = f32[1,128,128]{1,2,0:T(8,128)S(1)} custom-call(f32[1,128,128]{2,1,0:T(8,128)S(1)} %get-tuple-element.146), custom_call_target="InvertDiagBlocksLowerTriangular" | custom-call | tf_op jit(solution)/shard_map/jit(cholesky)/cholesky | solution.py:46
  30.9 11.7 %cholesky.147 = f32[128,128]{1,0:T(8,128)S(1)} custom-call(f32[128,128]{1,0:T(8,128)S(1)} %convolution_subtract_fusion.5), custom_call_target="Cholesky" | custom-call | tf_op jit(solution)/shard_map/jit(cholesky)/cholesky | solution.py:46
  44.5 0.7 fusion.38
  47.8 1.1 select_bitcast_fusion
  49.0 49.3 %all-reduce.11.cloned.1.call-done = f32[256,256]{1,0:T(8,128)} async-done(((f32[256,256]{1,0:T(8,128)}), f32[256,256]{1,0:T(8,128)}) %all-reduce.11.cloned.1.call-update) | async-done | bytes 262160 | tf_op jit(solution)/shard_map/psum | solution.py:11
  98.3 1.0 fusion.37
  99.3 3.7 while.5
  99.9 1.3 bitcast_dynamic-update-slice_fusion.13
  101.8 1.3 bitcast_dynamic-update-slice_fusion.13
  103.0 19.7 %custom-call.18 = f32[2,128,128]{1,2,0:T(8,128)S(1)} custom-call(f32[2,128,128]{2,1,0:T(8,128)S(1)} %get-tuple-element.29), custom_call_target="InvertDiagBlocksLowerTriangular" | custom-call | tf_op jit(solution)/shard_map/triangular_solve/custom-call.0 | solution.py:17
  124.2 0.9 bitcast_bitcast_fusion.1
  125.3 52.6 %all-reduce.19.cloned.1.call-done = (f32[4,256,128]{2,1,0:T(8,128)}, f32[4,256,128]{2,1,0:T(8,128)}) async-done(((f32[4,256,128]{2,1,0:T(8,128)}, f32[4,256,128]{2,1,0:T(8,128)}), (f32[4,256,128]{2,1,0:T(8,128)}, f32[4,256,128]{2,1,0:T(8,128)})) %all-reduce.19.cloned.1.call-update) | async-done | bytes 1048592 | tf_op jit(solution)/shard_map/psum | solution.py:11
  177.9 1.4 fusion.43
  179.3 2.3 dynamic-slice_select_fusion
  181.6 1.0 select_bitcast_fusion.26
  183.5 11.7 %cholesky.164 = f32[128,128]{1,0:T(8,128)S(1)} custom-call(f32[128,128]{1,0:T(8,128)S(1)} %cholesky.197), custom_call_target="Cholesky" | custom-call | tf_op jit(solution)/shard_map/jit(cholesky)/cholesky | solution.py:70
  195.3 9.8 %custom-call.19 = f32[1,128,128]{1,2,0:T(8,128)S(1)} custom-call(f32[1,128,128]{2,1,0:T(8,128)S(1)} %get-tuple-element.142), custom_call_target="InvertDiagBlocksLowerTriangular" | custom-call | tf_op jit(solution)/shard_map/jit(cholesky)/cholesky | solution.py:70
  205.6 11.7 %cholesky.181 = f32[128,128]{1,0:T(8,128)S(1)} custom-call(f32[128,128]{1,0:T(8,128)S(1)} %convolution_subtract_fusion.4), custom_call_target="Cholesky" | custom-call | tf_op jit(solution)/shard_map/jit(cholesky)/cholesky | solution.py:70
  220.0 0.7 select_select_fusion
  220.7 12.4 %all-reduce.17.cloned.1.call-start = ((), (), s32[]{:S(2)}) async-start(), calls=%async_computation.3 | async-start | bytes 3145728 | tf_op jit(solution)/shard_map/psum | solution.py:11
  233.1 40.8 %all-reduce.15.cloned.1.call-done = (f32[256,128]{1,0:T(8,128)}, f32[256,128]{1,0:T(8,128)}, f32[256,256]{1,0:T(8,128)}) async-done(((f32[256,128]{1,0:T(8,128)}, f32[256,128]{1,0:T(8,128)}, f32[256,256]{1,0:T(8,128)}), (f32[256,128]{1,0:T(8,128)}, f32[256,128]{1,0:T(8,128)}, f32[256,256]{1,0:T(8,128)})) %all-reduce.15.cloned.1.call-update) | async-done | bytes 524304 | tf_op jit(solution)/shard_map/psum | solution.py:11
  273.9 1.0 fusion.35
  275.0 4.0 while.6
  275.6 1.3 bitcast_dynamic-update-slice_fusion.14
  277.7 1.3 bitcast_dynamic-update-slice_fusion.14
  279.0 19.7 %custom-call.20 = f32[2,128,128]{1,2,0:T(8,128)S(1)} custom-call(f32[2,128,128]{2,1,0:T(8,128)S(1)} %get-tuple-element.30), custom_call_target="InvertDiagBlocksLowerTriangular" | custom-call | tf_op jit(solution)/shard_map/triangular_solve/custom-call.0 | solution.py:17
  300.0 1.0 fusion.46
  302.0 0.9 bitcast_bitcast_fusion
  302.8 1.4 fusion.12
  304.3 70.1 %all-reduce.17.cloned.1.call-done = (f32[4,256,128]{2,1,0:T(8,128)}, f32[4,256,128]{2,1,0:T(8,128)}, f32[4,256,128]{2,1,0:T(8,128)}) async-done(((f32[4,256,128]{2,1,0:T(8,128)}, f32[4,256,128]{2,1,0:T(8,128)}, f32[4,256,128]{2,1,0:T(8,128)}), (f32[4,256,128]{2,1,0:T(8,128)}, f32[4,256,128]{2,1,0:T(8,128)}, f32[4,256,128]{2,1,0:T(8,128)})) %all-reduce.17.cloned.1.call-update) | async-done | bytes 1572880 | tf_op jit(solution)/shard_map/psum | solution.py:11
  374.4 2.4 select_bitcast_fusion.2
  376.8 1.0 select_bitcast_fusion.3
  377.8 1.0 select_bitcast_fusion.4
  378.9 1.0 fusion.68
  381.3 1.0 fusion.69
  382.3 1.0 convolution_add_fusion
  383.3 113.3 %all-reduce.13.cloned.1.call-done = (f32[256,128]{1,0:T(8,128)}, f32[256,128]{1,0:T(8,128)}, f32[256,128]{1,0:T(8,128)}, f32[256,128]{1,0:T(8,128)}, f32[256,128...) async-done(((f32[256,128]{1,0:T(8,128)}, ...) | async-done | bytes 4980752 | tf_op jit(solution)/shard_map/psum | solution.py:11
  496.6 1.4 fusion.71
  498.1 1.4 fusion.28
  499.5 1.4 fusion.72
  501.0 1.4 fusion.73
  507.5 7.0 %fusion.7 = f32[8,256,4,256]{1,3,0,2:T(8,128)S(1)} fusion(f32[8,256,256]{2,1,0:T(8,128)S(1)} %fusion.14, f32[4,256,256]{2,1,0:T(8,128)S(1)} %convolution_add_fusion), kind=kOutput, calls=%fused_computation.13 | convolution fusion | flops 6442450944 | bytes 11534336 | tf_op jit(solution)/shard_map/lbk,mck->lmbc/dot_general | solution.py:100
  514.8 1.8 fusion.70
  516.6 9.3 %fusion.9 = f32[8,256,4,256]{1,3,0,2:T(8,128)} fusion(f32[8,256,256]{2,1,0:T(8,128)S(1)} %fusion.70, f32[4,256,256]{2,1,0:T(8,128)S(1)} %fusion.68), kind=kOutput, calls=%fused_computation.15 | convolution fusion | flops 6442450944 | bytes 11534336 | tf_op jit(solution)/shard_map/lbk,mck->lmbc/dot_general | solution.py:99
  525.9 12.9 %fusion.2 = f32[4,8,256,256]{3,2,1,0:T(8,128)} fusion(f32[8,256,4,256]{1,3,0,2:T(8,128)} %fusion.9, f32[8,256,4,256]{1,3,0,2:T(8,128)S(1)} %fusion.7, f32[4,256,256]{2,1,0:T(8,128)S(1)} %convolution_add_fusion, f32[4,256,256]{2,1,0:T(8,128)S(1)} %fusion.68, pred[8]{0:T(512)(128)(4,1)S(1)} %get-tuple-element.153, pred[8]{0:T(512)(128)(4,1)S(1)} %get-tuple-element.154, ...), kind=kOutput, calls=%fused_computation.9 | convolution fusion | flops 3233808384 | bytes 31461424 | tf_op jit(solution)/shard_map/lmbr,lmcr->lmbc/dot_general | solution.py:98
  (184 shorter events, 19.2 us)
Async XLA Ops:
  6.5 39.3 %copy-start = (s32[32,32]{1,0:T(8,128)S(1)}, s32[32,32]{1,0:T(8,128)}, u32[]{:S(2)}) copy-start(s32[32,32]{1,0:T(8,128)} %param.10) | copy-start | bytes 12292
  6.5 91.7 %all-reduce.11.cloned.1.call-start = ((), (), s32[]{:S(2)}) async-start(), calls=%async_computation | async-start | bytes 524288 | tf_op jit(solution)/shard_map/psum | solution.py:11
  6.5 39.1 %slice-start = ((bf16[4,8,256,128]{3,2,1,0:T(8,128)(2,1)}), bf16[4,1,256,128]{3,2,1,0:T(8,128)(2,1)S(1)}, s32[]{:S(2)}) async-start(bf16[4,8,256,128]{3,2,1,0:T(8,128)(2,1)} %param.9), calls=%async_computation.5 | async-start | bytes 524288 | tf_op jit(solution)/shard_map/slice | solution.py:47
  7.7 39.6 %copy-start.4 = (bf16[4,8,256,128]{3,2,1,0:T(8,128)(2,1)S(1)}, bf16[4,8,256,128]{3,2,1,0:T(8,128)(2,1)}, u32[]{:S(2)}) copy-start(bf16[4,8,256,128]{3,2,1,0:T(8,128)(2,1)} %param.8) | copy-start | bytes 6291460
  45.3 132.6 %all-reduce.19.cloned.1.call-start = ((), (), s32[]{:S(2)}) async-start(), calls=%async_computation.4 | async-start | bytes 2097152 | tf_op jit(solution)/shard_map/psum | solution.py:11
  125.0 148.9 %all-reduce.15.cloned.1.call-start = ((), (), s32[]{:S(2)}) async-start(), calls=%async_computation.2 | async-start | bytes 1048576 | tf_op jit(solution)/shard_map/psum | solution.py:11
  177.9 3.7 copy-start.2
  205.3 94.6 %copy-start.3 = (f32[4,256,128]{2,1,0:T(8,128)S(1)}, f32[4,256,128]{2,1,0:T(8,128)}, u32[]{:S(2)}) copy-start(f32[4,256,128]{2,1,0:T(8,128)} %get-tuple-element.92) | copy-start | bytes 1572868
  220.7 153.7 %all-reduce.17.cloned.1.call-start = ((), (), s32[]{:S(2)}) async-start(), calls=%async_computation.3 | async-start | bytes 3145728 | tf_op jit(solution)/shard_map/psum | solution.py:11
  273.9 25.2 %copy-start.10 = (f32[256,128]{1,0:T(8,128)S(1)}, f32[256,128]{1,0:T(8,128)}, u32[]{:S(2)}) copy-start(f32[256,128]{1,0:T(8,128)} %get-tuple-element.85) | copy-start | bytes 393220
  273.9 26.0 %copy-start.11 = (f32[256,128]{1,0:T(8,128)S(1)}, f32[256,128]{1,0:T(8,128)}, u32[]{:S(2)}) copy-start(f32[256,128]{1,0:T(8,128)} %get-tuple-element.86) | copy-start | bytes 393220
  304.3 192.3 %all-reduce.13.cloned.1.call-start = ((), (), s32[]{:S(2)}) async-start(), calls=%async_computation.1 | async-start | bytes 9961472 | tf_op jit(solution)/shard_map/psum | solution.py:11
  374.4 2.4 copy-start.7
  374.4 3.4 copy-start.6
  378.9 3.3 copy-start.5
  496.6 5.8 %copy-start.41 = (f32[256,128]{1,0:T(8,128)S(1)}, f32[256,128]{1,0:T(8,128)}, u32[]{:S(2)}) copy-start(f32[256,128]{1,0:T(8,128)} %get-tuple-element.70) | copy-start | bytes 393220
  496.6 5.8 %copy-start.42 = (f32[256,128]{1,0:T(8,128)S(1)}, f32[256,128]{1,0:T(8,128)}, u32[]{:S(2)}) copy-start(f32[256,128]{1,0:T(8,128)} %get-tuple-element.71) | copy-start | bytes 393220
  496.6 6.2 %copy-start.39 = (f32[256,128]{1,0:T(8,128)S(1)}, f32[256,128]{1,0:T(8,128)}, u32[]{:S(2)}) copy-start(f32[256,128]{1,0:T(8,128)} %get-tuple-element.73) | copy-start | bytes 393220
  496.6 6.2 %copy-start.40 = (f32[256,128]{1,0:T(8,128)S(1)}, f32[256,128]{1,0:T(8,128)}, u32[]{:S(2)}) copy-start(f32[256,128]{1,0:T(8,128)} %get-tuple-element.74) | copy-start | bytes 393220
  496.6 6.6 %copy-start.37 = (f32[256,128]{1,0:T(8,128)S(1)}, f32[256,128]{1,0:T(8,128)}, u32[]{:S(2)}) copy-start(f32[256,128]{1,0:T(8,128)} %get-tuple-element.76) | copy-start | bytes 393220
  496.6 6.6 %copy-start.38 = (f32[256,128]{1,0:T(8,128)S(1)}, f32[256,128]{1,0:T(8,128)}, u32[]{:S(2)}) copy-start(f32[256,128]{1,0:T(8,128)} %get-tuple-element.77) | copy-start | bytes 393220
  496.6 7.0 %copy-start.35 = (f32[256,128]{1,0:T(8,128)S(1)}, f32[256,128]{1,0:T(8,128)}, u32[]{:S(2)}) copy-start(f32[256,128]{1,0:T(8,128)} %get-tuple-element.79) | copy-start | bytes 393220
  496.6 7.0 %copy-start.36 = (f32[256,128]{1,0:T(8,128)S(1)}, f32[256,128]{1,0:T(8,128)}, u32[]{:S(2)}) copy-start(f32[256,128]{1,0:T(8,128)} %get-tuple-element.80) | copy-start | bytes 393220
  498.1 5.9 %copy-start.33 = (f32[256,128]{1,0:T(8,128)S(1)}, f32[256,128]{1,0:T(8,128)}, u32[]{:S(2)}) copy-start(f32[256,128]{1,0:T(8,128)} %get-tuple-element.82) | copy-start | bytes 393220
  498.1 5.9 %copy-start.34 = (f32[256,128]{1,0:T(8,128)S(1)}, f32[256,128]{1,0:T(8,128)}, u32[]{:S(2)}) copy-start(f32[256,128]{1,0:T(8,128)} %get-tuple-element.83) | copy-start | bytes 393220
  498.1 6.3 %copy-start.9 = (f32[8,256,128]{2,1,0:T(8,128)S(1)}, f32[8,256,128]{2,1,0:T(8,128)}, u32[]{:S(2)}) copy-start(f32[8,256,128]{2,1,0:T(8,128)} %bitcast_dynamic-update-slice_fusion.10) | copy-start | bytes 3145732
  498.1 6.3 %copy-start.18 = (f32[256,128]{1,0:T(8,128)S(1)}, f32[256,128]{1,0:T(8,128)}, u32[]{:S(2)}) copy-start(f32[256,128]{1,0:T(8,128)} %get-tuple-element.47) | copy-start | bytes 393220
  499.5 5.0 copy-start.17
  499.5 5.0 copy-start.16
  500.9 3.6 copy-start.15
  500.9 3.6 copy-start.14
  502.4 2.3 copy-start.13
  502.4 2.3 copy-start.12
  502.8 1.9 copy-start.32
  503.2 1.9 copy-start.31
  504.0 1.5 copy-start.30
  504.6 1.7 copy-start.28
  504.7 2.0 copy-start.27
  505.1 2.0 copy-start.26
  507.5 7.1 %copy-start.8 = (f32[8,256,128]{2,1,0:T(8,128)S(1)}, f32[8,256,128]{2,1,0:T(8,128)}, u32[]{:S(2)}) copy-start(f32[8,256,128]{2,1,0:T(8,128)} %bitcast_dynamic-update-slice_fusion.2) | copy-start | bytes 3145732
  507.5 7.1 %copy-start.25 = (f32[1,256,128]{2,1,0:T(8,128)S(1)}, f32[1,256,128]{2,1,0:T(8,128)}, u32[]{:S(2)}) copy-start(f32[1,256,128]{2,1,0:T(8,128)} %get-tuple-element.54) | copy-start | bytes 393220
  507.5 7.1 %copy-start.24 = (f32[1,256,128]{2,1,0:T(8,128)S(1)}, f32[1,256,128]{2,1,0:T(8,128)}, u32[]{:S(2)}) copy-start(f32[1,256,128]{2,1,0:T(8,128)} %get-tuple-element.55) | copy-start | bytes 393220
  507.5 7.2 %copy-start.23 = (f32[1,256,128]{2,1,0:T(8,128)S(1)}, f32[1,256,128]{2,1,0:T(8,128)}, u32[]{:S(2)}) copy-start(f32[1,256,128]{2,1,0:T(8,128)} %get-tuple-element.56) | copy-start | bytes 393220
  507.5 7.2 %copy-start.22 = (f32[1,256,128]{2,1,0:T(8,128)S(1)}, f32[1,256,128]{2,1,0:T(8,128)}, u32[]{:S(2)}) copy-start(f32[1,256,128]{2,1,0:T(8,128)} %get-tuple-element.57) | copy-start | bytes 393220
  507.5 7.2 %copy-start.21 = (f32[1,256,128]{2,1,0:T(8,128)S(1)}, f32[1,256,128]{2,1,0:T(8,128)}, u32[]{:S(2)}) copy-start(f32[1,256,128]{2,1,0:T(8,128)} %get-tuple-element.58) | copy-start | bytes 393220
  507.5 7.2 %copy-start.20 = (f32[1,256,128]{2,1,0:T(8,128)S(1)}, f32[1,256,128]{2,1,0:T(8,128)}, u32[]{:S(2)}) copy-start(f32[1,256,128]{2,1,0:T(8,128)} %get-tuple-element.59) | copy-start | bytes 393220
  507.5 7.2 %copy-start.19 = (f32[1,256,128]{2,1,0:T(8,128)S(1)}, f32[1,256,128]{2,1,0:T(8,128)}, u32[]{:S(2)}) copy-start(f32[1,256,128]{2,1,0:T(8,128)} %get-tuple-element.60) | copy-start | bytes 393220
  525.9 13.0 %copy-start.1 = (s32[32,32]{1,0:T(8,128)S(1)}, s32[32,32]{1,0:T(8,128)}, u32[]{:S(2)}) copy-start(s32[32,32]{1,0:T(8,128)} %param.10) | copy-start | bytes 12292
  (1 other events, 1.4 us)
Sparse Core Ops, SparseCore 0:
  45.4 52.7 all-reduce.10
  125.2 52.6 all-reduce.18
  220.9 53.0 all-reduce.14
  304.4 69.9 all-reduce.16
  381.8 114.7 all-reduce.12
where the time goes:
time: 556 us; the launch traced here: 546 us
  waiting for transfers between devices  326 us (59%)
  other arithmetic  124 us (22%)
  matrix products  53.2 us (10%)
  between operations  17.4 us (3%)
  starting transfers between devices  12.8 us (2%)
  local copies, waits for them, and re-layouts  12.1 us (2%)
    psum x5, waiting for transfers between devices, from_root(): return lax.psum(jnp.where(mine, shard, jnp.zeros_like(shard)), axis)  326 us
    another operation x5, other arithmetic, lower_solve(): lax.linalg.triangular_solve(factor, flattened, left_side=True, lower=True)  41.3 us
    another operation x7, other arithmetic, shards(): second_pivot = from_root(jnp.linalg.cholesky(shifted), 'row', 1)  34.7 us
    another operation x6, other arithmetic, shards(): first_pivot = from_root(jnp.linalg.cholesky(diag_tiles[0]), 'row', 0)  33.9 us
    dot_general x20, matrix products, expand(): return jnp.einsum('nbr,ncr->nbc', left_basis, weights, precision=PRECISE)  14.9 us
    dot_general x1, matrix products, shards(): jnp.einsum('lmbr,lmcr->lmbc', left_bases, right_coefs, precision=PRECISE)  12.9 us
    psum x5, starting transfers between devices, from_root(): return lax.psum(jnp.where(mine, shard, jnp.zeros_like(shard)), axis)  12.8 us
    select_n x10, other arithmetic, from_root(): return lax.psum(jnp.where(mine, shard, jnp.zeros_like(shard)), axis)  11.9 us
  transfers between devices with their start and end apart: 5, of which 5 were waited for; matrix products, arithmetic and copies ran while one was open for 1% of the time, Pallas kernels for 0%

commit v1 on v0

v1 whole, which is shorter than its diff:
```python
import functools

import jax
import jax.numpy as jnp
from jax import lax
from jax.experimental import pallas as pl
from jax.experimental.pallas import tpu as pltpu
from jax.sharding import PartitionSpec as P

PRECISE = lax.Precision.HIGHEST
AXES = ("row", "col")
BLOCK = 32
GROUP = 8
LANES = 128
NT = (((1,), (1,)), ((), ()))
TN = (((0,), (0,)), ((), ()))
NN = (((1,), (0,)), ((), ()))
ANYWHERE = pl.BlockSpec(memory_space=pl.ANY)
IN_VMEM = pl.BlockSpec(memory_space=pltpu.VMEM)
IN_SMEM = pl.BlockSpec(memory_space=pltpu.SMEM)
VMEM_LIMIT = 48 * 1024 * 1024


def dot32(lhs, rhs, dims):
    return lax.dot_general(lhs, rhs, dims, precision=PRECISE, preferred_element_type=jnp.float32)


def dot16(lhs, rhs, dims):
    return lax.dot_general(lhs, rhs, dims, preferred_element_type=jnp.float32)


def split2(value):
    high = value.astype(jnp.bfloat16)
    low = (value - high.astype(jnp.float32)).astype(jnp.bfloat16)
    return high, low


def split3(value):
    high = value.astype(jnp.bfloat16)
    rest = value - high.astype(jnp.float32)
    middle = rest.astype(jnp.bfloat16)
    low = (rest - middle.astype(jnp.float32)).astype(jnp.bfloat16)
    return high, middle, low


def params(**extra):
    return pltpu.CompilerParams(vmem_limit_bytes=VMEM_LIMIT, **extra)


def cost(flops, moved):
    return pl.CostEstimate(flops=int(flops), bytes_accessed=int(moved), transcendentals=0)


def eliminate(tiles):
    tiles, start = tiles
    rows = tiles[0].shape[0]
    done = []
    for first in range(0, rows, GROUP):
        height = rows - first
        row_ids = lax.broadcasted_iota(jnp.int32, (height, LANES), 0)
        heads = [
            jnp.broadcast_to(tiles[0][:, start + first + j : start + first + j + 1], (height, LANES))
            for j in range(GROUP)
        ]
        scale = jnp.zeros((GROUP, LANES), jnp.float32)
        for j in range(GROUP):
            pivot = heads[j][j : j + 1, :]
            factor = jnp.where(row_ids > j, heads[j] * (1.0 / pivot), 0.0)
            for other in range(j + 1, GROUP):
                heads[other] = heads[other] - factor * heads[other][j : j + 1, :]
            tiles = [tile - factor * tile[j : j + 1, :] for tile in tiles]
            root = lax.rsqrt(pivot)
            root = root * (1.5 - 0.5 * pivot * root * root)
            scale = jnp.where(row_ids[:GROUP] == j, root, scale)
        done.append([tile[:GROUP] * scale for tile in tiles])
        tiles = [tile[GROUP:] for tile in tiles]
    return [jnp.concatenate(parts, axis=0) for parts in zip(*done)]


def inverse_factor(source, work, result):
    order = source.shape[0]
    span = order // LANES
    for base in range(0, order, BLOCK):
        low = base // LANES
        row_ids = lax.broadcasted_iota(jnp.int32, (BLOCK, LANES), 0)
        lane_ids = lax.broadcasted_iota(jnp.int32, (BLOCK, LANES), 1)
        unit = jnp.where(lane_ids - base % LANES == row_ids, 1.0, 0.0)
        zero = jnp.zeros((BLOCK, LANES), jnp.float32)
        tiles = [source[base : base + BLOCK, s * LANES : (s + 1) * LANES] for s in range(low, span)]
        tiles += [zero] * low + [unit]
        if base:
            taken = dot32(
                work[0:base, base : base + BLOCK],
                work[0:base, low * LANES : order + (low + 1) * LANES],
                TN,
            )
            tiles = [tile - taken[:, s * LANES : (s + 1) * LANES] for s, tile in enumerate(tiles)]
        tiles = eliminate((tiles, base % LANES))
        for s, tile in enumerate(tiles):
            work[base : base + BLOCK, (low + s) * LANES : (low + s + 1) * LANES] = tile
        for s in range(low + 1, span):
            work[base : base + BLOCK, order + s * LANES : order + (s + 1) * LANES] = zero
    result[...] = work[:, order:]


def first_kernel(tile, result, work):
    inverse_factor(tile, work, result)


def first_inverse(tile):
    order = tile.shape[0]
    return pl.pallas_call(
        first_kernel,
        out_shape=jax.ShapeDtypeStruct((order, order), jnp.float32),
        in_specs=[IN_VMEM],
        out_specs=IN_VMEM,
        scratch_shapes=[pltpu.VMEM((order, 2 * order), jnp.float32)],
        compiler_params=params(),
        cost_estimate=cost(2**33, 2**20),
        name="first_inverse",
    )(tile)


def second_kernel(rank, head, inverse, result, mixing, shifted, work):
    order = inverse.shape[0]
    cap = (head.shape[0] - order) // 2
    live = lax.broadcasted_iota(jnp.int32, (cap, order), 0) < rank[0]
    left = jnp.where(live, head[order : order + cap, :], 0.0)
    right = jnp.where(live, head[order + cap :, :], 0.0)
    solved = dot32(right, inverse[...], NT)
    dense = dot32(left, solved, TN)
    shifted[...] = head[0:order, :] - dot32(dense, dense, NT)
    inverse_factor(shifted, work, result)
    mixing[...] = -dot32(dot32(result[...], dense, NN), inverse[...], NN)


def second_inverse(rank, head, inverse):
    order = inverse.shape[0]
    shape = jax.ShapeDtypeStruct((order, order), jnp.float32)
    return pl.pallas_call(
        second_kernel,
        out_shape=(shape, shape),
        in_specs=[IN_SMEM, IN_VMEM, IN_VMEM],
        out_specs=(IN_VMEM, IN_VMEM),
        scratch_shapes=[
            pltpu.VMEM((order, order), jnp.float32),
            pltpu.VMEM((order, 2 * order), jnp.float32),
        ],
        compiler_params=params(),
        cost_estimate=cost(2**33, 2**20),
        name="second_inverse",
    )(rank, head, inverse)


def pack_kernel(capacity, offsets, ranks, left, right, left_out, right_out):
    slots, _, order, cap = left.shape
    place = lax.broadcasted_iota(jnp.int32, (capacity, cap), 0)
    column = lax.broadcasted_iota(jnp.int32, (capacity, cap), 1)
    for source, target in ((left, left_out), (right, right_out)):
        total = jnp.zeros((capacity, order), jnp.float32)
        for slot in range(slots):
            hit = (place - offsets[slot] == column) & (column < ranks[slot])
            chosen = jnp.where(hit, 1.0, 0.0).astype(jnp.bfloat16)
            total = total + dot16(chosen, source[slot, 0], NT)
        target[...] = total


def pack(left_fac, right_fac, offsets, ranks, capacity):
    slots, _, order, cap = left_fac.shape
    shape = jax.ShapeDtypeStruct((capacity, order), jnp.float32)
    block = pl.BlockSpec((slots, 1, order, cap), lambda step: (0, 0, 0, 0))
    whole = pl.BlockSpec((capacity, order), lambda step: (0, 0))
    return pl.pallas_call(
        functools.partial(pack_kernel, capacity),
        grid=(1,),
        out_shape=(shape, shape),
        in_specs=[IN_SMEM, IN_SMEM, block, block],
        out_specs=(whole, whole),
        compiler_params=params(),
        cost_estimate=cost(2**28, 2**20),
        name="pack",
    )(offsets, ranks, left_fac, right_fac)


def panel_kernel(capacity, groups, factors, choice, offsets, ranks, *refs):
    total = sum(sum(counts) for counts in groups)
    sources, (first, second, mixing) = refs[:total], refs[total : total + 3]
    high_out, low_out = refs[total + 3 : total + 5]
    landed, weight_high, weight_low, sems = refs[total + 5 :]
    order = first.shape[0]
    cap = LANES
    slots = offsets.shape[1] // 2
    at = 0
    waits = []
    for g, counts in enumerate(groups):
        for k, count in enumerate(counts):
            candidates = sources[at : at + count]
            at += count
            spot = landed.at[4 * g + k, pl.ds(0, capacity)]
            for n, candidate in enumerate(candidates):
                copy = pltpu.make_async_copy(candidate, spot, sems.at[4 * g + k])
                if count == 1:
                    copy.start()
                else:
                    pl.when(choice[4 * g + k] == n)(copy.start)
            waits.append(pltpu.make_async_copy(candidates[0], spot, sems.at[4 * g + k]))
            landed[4 * g + k, capacity:, :] = jnp.zeros((cap, order), jnp.float32)
    base = jnp.concatenate([first[...], mixing[...]], axis=0)
    base_parts, second_parts = split3(base), split3(second[...])
    for wait in waits:
        wait.wait()
    for g in range(len(groups)):
        right0 = landed[4 * g + 1].astype(jnp.bfloat16)
        right1 = landed[4 * g + 3].astype(jnp.bfloat16)
        solved0 = sum(dot16(right0, part, NT) for part in base_parts)
        solved1 = sum(dot16(right1, part, NT) for part in second_parts)
        for column, value in ((0, solved0), (2 * order, solved1)):
            high, low = split2(value)
            weight_high[:, column : column + value.shape[1]] = high
            weight_low[:, column : column + value.shape[1]] = low
        live = lax.broadcasted_iota(jnp.int32, (cap, order), 0)
        for slot in range(slots):
            pieces = []
            for k in range(2):
                spot = pl.ds(pl.multiple_of(offsets[g, k * slots + slot], 16), cap)
                left = landed[4 * g + 2 * k, spot, :]
                left = jnp.where(live < ranks[g, k * slots + slot], left, 0.0).astype(jnp.bfloat16)
                columns = pl.ds(0, 2 * order) if k == 0 else pl.ds(2 * order, order)
                weights = jnp.concatenate([weight_high[spot, columns], weight_low[spot, columns]], axis=0)
                pieces.append(dot16(jnp.concatenate([left, left], axis=0), weights, TN))
            panel0 = pieces[0][:, :order]
            panel1 = pieces[0][:, order:] + pieces[1]
            where = slot if factors is None else slot * factors + choice[4 * len(groups) + g]
            for column, value in ((0, panel0), (order, panel1)):
                high, low = split2(value)
                high_out[where, :, column : column + order] = high
                low_out[where, :, column : column + order] = low


def panels(groups, choice, offsets, ranks, inverses, capacity, name):
    order = inverses[0].shape[0]
    count = len(groups)
    slots = offsets.shape[1] // 2
    flat = [array for group in groups for candidates in group for array in candidates]
    counts = tuple(tuple(len(candidates) for candidates in group) for group in groups)
    shape = jax.ShapeDtypeStruct((slots * count, order, 2 * order), jnp.bfloat16)
    return pl.pallas_call(
        functools.partial(panel_kernel, capacity, counts, count if count > 1 else None),
        out_shape=(shape, shape),
        in_specs=[IN_SMEM] * 3 + [ANYWHERE] * len(flat) + [IN_VMEM] * 3,
        out_specs=(IN_VMEM, IN_VMEM),
        scratch_shapes=[
            pltpu.VMEM((4 * count, capacity + LANES, order), jnp.float32),
            pltpu.VMEM((capacity + LANES, 3 * order), jnp.bfloat16),
            pltpu.VMEM((capacity + LANES, 3 * order), jnp.bfloat16),
            pltpu.SemaphoreType.DMA((4 * count,)),
        ],
        compiler_params=params(),
        cost_estimate=cost(2**31 * count, 2**22 * count),
        name=name,
    )(choice, offsets, ranks, *flat, *inverses)


def schur_kernel(place, ranks, left, right, row_high, row_low, col_high, col_low, out):
    row_slot, col_slot = pl.program_id(0), pl.program_id(1)
    tile_row = row_slot * place[2] + place[0]
    tile_col = col_slot * place[3] + place[1]
    order = out.shape[2]

    @pl.when(tile_row <= tile_col)
    def _():
        out[0, 0] = jnp.zeros((order, order), jnp.float32)

    @pl.when((tile_row > tile_col) & (tile_col == 0))
    def _():
        out[0, 0] = row_high[row_slot, :, :order].astype(jnp.float32) + row_low[row_slot, :, :order].astype(jnp.float32)

    @pl.when((tile_row > tile_col) & (tile_col == 1))
    def _():
        out[0, 0] = row_high[row_slot, :, order:].astype(jnp.float32) + row_low[row_slot, :, order:].astype(jnp.float32)

    @pl.when((tile_row > tile_col) & (tile_col > 1))
    def _():
        basis = left[0, 0]
        live = lax.broadcasted_iota(jnp.int32, basis.shape, 1) < ranks[row_slot, col_slot]
        basis = jnp.where(live, basis.astype(jnp.float32), 0.0).astype(jnp.bfloat16)
        front = dot16(basis, right[0, 0], NT)
        high, low = row_high[row_slot], row_low[row_slot]
        update = dot16(high, col_high[col_slot], NT)
        update = update + dot16(high, col_low[col_slot], NT)
        update = update + dot16(low, col_high[col_slot], NT)
        out[0, 0] = front - update


def schur(place, ranks, left_fac, right_fac, rows, cols):
    row_slots, col_slots, order, cap = left_fac.shape
    factor = pl.BlockSpec((1, 1, order, cap), lambda a, m: (a, m, 0, 0))
    return pl.pallas_call(
        schur_kernel,
        grid=(row_slots, col_slots),
        out_shape=jax.ShapeDtypeStruct((row_slots, col_slots, order, order), jnp.float32),
        in_specs=[IN_SMEM, IN_SMEM, factor, factor] + [IN_VMEM] * 4,
        out_specs=pl.BlockSpec((1, 1, order, order), lambda a, m: (a, m, 0, 0)),
        compiler_params=params(dimension_semantics=("arbitrary", "arbitrary")),
        cost_estimate=cost(2**33, 2**24),
        name="schur",
    )(place, ranks, left_fac, right_fac, *rows, *cols)


def shards(diag_tiles, left_fac, right_fac, ranks):
    grid_rows = lax.axis_size("row")
    grid_cols = lax.axis_size("col")
    row_here = lax.axis_index("row")
    col_here = lax.axis_index("col")
    row_slots, col_slots, order, cap = left_fac.shape
    assert cap == LANES and grid_rows % grid_cols == 0 and grid_cols >= 2
    spread = grid_rows // grid_cols
    row_bits = grid_rows.bit_length() - 1
    low_bits = grid_cols.bit_length() - 1
    assert 1 << row_bits == grid_rows and 1 << low_bits == grid_cols
    capacity = row_slots * cap

    def move(array, pairs):
        flat = [(r * grid_cols + c, s * grid_cols + d) for (r, c), (s, d) in pairs]
        return lax.ppermute(array, AXES, flat)

    every_row = range(grid_rows)
    every_col = range(grid_cols)

    tile_ids = jnp.arange(ranks.shape[0], dtype=jnp.int32)
    panel_ranks = jnp.stack([jnp.where(tile_ids > t, ranks[:, t], 0) for t in range(2)])
    panel_ranks = panel_ranks.reshape(2, row_slots, grid_rows)
    starts = jnp.broadcast_to(jnp.arange(row_slots, dtype=jnp.int32)[None, :, None] * cap, panel_ranks.shape)

    def of_group(table, group):
        return lax.dynamic_index_in_dim(table, group, 2, keepdims=False)

    my_ranks = of_group(panel_ranks, row_here)
    my_starts = of_group(starts, row_here)
    panel_here = jnp.minimum(col_here, 1)
    left_pack, right_pack = pack(
        left_fac,
        right_fac,
        lax.dynamic_index_in_dim(my_starts, panel_here, 0, keepdims=False),
        lax.dynamic_index_in_dim(my_ranks, panel_here, 0, keepdims=False),
        capacity,
    )

    tree_bits = list(range(1, row_bits)) + [0]

    def spread_rows(array, root):
        held = [root]
        for bit in tree_bits:
            step = 1 << bit
            got = move(array, [((r, c), (r ^ step, c)) for r in held for c in every_col])
            mask = sum(1 << b for b in range(row_bits) if all((h ^ root) >> b & 1 == 0 for h in held) and b != bit)
            arrived = (((row_here ^ root) & mask) == 0) & (((row_here ^ root) >> bit) & 1 == 1)
            array = jnp.where(arrived, got, array)
            held = held + [r ^ step for r in held]
        return array

    first_tile = spread_rows(diag_tiles[0], 0)

    pivot_bases = jnp.concatenate([left_pack[:cap], right_pack[:cap]], axis=0)
    received = [move(pivot_bases, [((1, 0), (1, c))]) for c in every_col if c]
    pivot_bases = jnp.where(col_here == 0, pivot_bases, sum(received))
    head = spread_rows(jnp.concatenate([diag_tiles[0], pivot_bases], axis=0), 1)

    chains = []
    for array in (left_pack, right_pack):
        back = move(array, [((r, 1), (r, 0)) for r in every_row])
        chain = [array]
        for s in range(1, grid_cols):
            pairs = [((r, c - 1), (r, c)) for c in (s, s + 1) if c < grid_cols for r in every_row]
            chain.append(move(chain[-1], pairs))
        chains.append((chain, back))

    def pick(index, arrays):
        out = arrays[0]
        for n in range(1, len(arrays)):
            out = jnp.where(index == n, arrays[n], out)
        return out

    row_arrays = []
    for t in range(2):
        for chain, back in chains:
            row_arrays.append(chain if t == 0 else [back] + chain[:-1])

    inverse0 = first_inverse(first_tile)
    inverse1, mixing = second_inverse(ranks[1, 0][None], head, inverse0)
    inverses = (inverse0, inverse1, mixing)

    col_arrays = []
    for candidates in row_arrays:
        have = pick(col_here, candidates)
        held = {c: [c] for c in every_col}
        for bit in range(1, low_bits):
            step = 1 << bit
            pairs = [((r + h * grid_cols, c), ((r ^ step) + h * grid_cols, c)) for c in every_col for r in held[c] for h in range(spread)]
            got = move(have, pairs)
            mask = (grid_cols - 1) - sum(1 << b for b in range(1, bit + 1))
            offset = (row_here ^ col_here) & (grid_cols - 1)
            arrived = ((offset & mask) == 0) & ((offset >> bit) & 1 == 1)
            have = jnp.where(arrived, got, have)
            held = {c: held[c] + [r ^ step for r in held[c]] for c in every_col}
        sets = [have]
        for bit in range(low_bits, row_bits):
            step = 1 << bit
            pairs = [((r + h * grid_cols, c), ((r + h * grid_cols) ^ step, c)) for c in every_col for r in held[c] for h in range(spread)]
            sets = sets + [move(array, pairs) for array in sets]
        pairs = [((r + h * grid_cols, c), ((r ^ 1) + h * grid_cols, c)) for c in every_col for r in held[c] for h in range(spread)]
        col_arrays.append([[array, move(array, pairs)] for array in sets])

    row_group = my_starts.reshape(1, -1), my_ranks.reshape(1, -1)
    rows = panels(
        [row_arrays],
        jnp.full((5,), col_here, jnp.int32),
        *row_group,
        inverses,
        capacity,
        "row_panels",
    )
    mine = row_here // grid_cols
    groups = [(mine ^ g) * grid_cols + col_here for g in range(spread)]
    col_starts = jnp.stack([of_group(starts, group).reshape(-1) for group in groups])
    col_ranks = jnp.stack([of_group(panel_ranks, group).reshape(-1) for group in groups])
    passed = (row_here ^ col_here) & 1
    choice = jnp.concatenate(
        [jnp.full((4 * spread,), passed, jnp.int32), jnp.stack([mine ^ g for g in range(spread)]).astype(jnp.int32)]
    )
    cols = panels(
        [[col_arrays[k][g] for k in range(4)] for g in range(spread)],
        choice,
        col_starts,
        col_ranks,
        inverses,
        capacity,
        "col_panels",
    )
    place = jnp.stack([row_here, col_here, jnp.int32(grid_rows), jnp.int32(grid_cols)]).astype(jnp.int32)
    tile_rows = jnp.arange(row_slots, dtype=jnp.int32) * grid_rows + row_here
    tile_cols = jnp.arange(col_slots, dtype=jnp.int32) * grid_cols + col_here
    local_ranks = jnp.take(jnp.take(ranks, tile_rows, axis=0), tile_cols, axis=1)
    return schur(place, local_ranks, left_fac, right_fac, rows, cols)


def solution(mesh):
    in_specs = (P("row", None, None), P("row", "col", None, None), P("row", "col", None, None), P())
    out_specs = P("row", "col", None, None)
    return jax.shard_map(shards, mesh=mesh, in_specs=in_specs, out_specs=out_specs, check_vma=False)
```

time: 556 us -> 169 us (0.30)
  the two profiles are of different devices: /device:TPU:21 before, /device:TPU:16 now
where the time goes in v1:
time: 169 us; the launch traced here: 167 us
  Pallas kernels  55.9 us (33%)
  starting transfers between devices  53.6 us (32%)
  waiting for transfers between devices  38.3 us (23%)
  other arithmetic  9.87 us (6%)
  local copies, waits for them, and re-layouts  8.67 us (5%)
    ppermute x33, starting transfers between devices, move(): return lax.ppermute(array, AXES, flat)  53.6 us
    ppermute x33, waiting for transfers between devices, move(): return lax.ppermute(array, AXES, flat)  38.3 us
    pallas_call x1, Pallas kernels, schur(): pl.pallas_call(schur_kernel, grid=(row_slots, col_slots), out_shape=jax.S...  21.6 us
    pallas_call x2, Pallas kernels, panels(): pl.pallas_call(functools.partial(panel_kernel, capacity, counts, count if...  12.7 us
    pallas_call x1, Pallas kernels, second_inverse(): pl.pallas_call(second_kernel, out_shape=(shape, shape), in_specs=[IN_SMEM...  11.7 us
    pallas_call x1, Pallas kernels, first_inverse(): pl.pallas_call(first_kernel, out_shape=jax.ShapeDtypeStruct((order, order...  8.57 us
    select_n x6, other arithmetic, spread_rows(): array = jnp.where(arrived, got, array)  5.56 us
    unnamed x26, local copies, waits for them, and re-layouts  4.4 us
  transfers between devices with their start and end apart: 33, of which 10 were waited for; matrix products, arithmetic and copies ran while one was open for 8% of the time, Pallas kernels for 15%

profile of v1, /device:TPU:16, one launch (start us, length us, event | category | flops | bytes accessed | tf_op | source)
XLA Modules:
  0.0 167.0 jit_solution(16424419297928098450)
XLA Ops:
  1.4 1.6 copy-done
  3.0 1.6 copy-done.2
  7.2 1.4 collective-permute-start.11
  8.6 1.3 collective-permute-start.3
  10.9 4.1 %collective-permute-start.8 = (f32[256,256]{1,0:T(8,128)S(1)}, f32[256,256]{1,0:T(8,128)}, u32[]{:S(2)}, u32[]{:S(2)}) collective-permute-start(f32[256,256]{1,0:T(8,128)S(1)} %slice_bitcast_fusion), channel_id=1, source_target_pairs={{0,8},{1,9},{2,10},{3,11}} | collective-permute-start | bytes 786440 | tf_op jit(solution)/shard_map/ppermute | solution.py:325
  16.5 1.6 collective-permute-done.8
  18.1 1.3 collective-permute-start
  19.4 1.7 %broadcast_select_fusion.7 = f32[256,256]{1,0:T(8,128)} fusion(f32[256,256]{1,0:T(8,128)} %collective-permute-done.8, pred[]{:T(512)S(6)} %and.98, f32[4,256,256]{2,1,0:T(8,128)} %param.4), kind=kLoop, calls=%fused_computation.17 | loop fusion | flops 65536 | bytes 786433 | tf_op jit(solution)/shard_map/jit(_where)/select_n | solution.py:358
  21.1 1.5 collective-permute-start.7
  22.6 2.0 %collective-permute-start.9 = (f32[256,256]{1,0:T(8,128)}, f32[256,256]{1,0:T(8,128)}, u32[]{:S(2)}, u32[]{:S(2)}) collective-permute-start(f32[256,256]{1,0:T(8,128)} %broadcast_select_fusion.7), channel_id=1, source_target_pairs={{0,16},{1,17},{2,18},{3,19},{8,24},{9,25},{10,26},{11,27}} | collective-permute-start | bytes 786440 | tf_op jit(solution)/shard_map/ppermute | solution.py:325
  25.6 3.4 %collective-permute-done.3.refs_5_.refs_14_ = f32[512,256]{1,0:T(8,128)S(1)} collective-permute-done((f32[512,256]{1,0:T(8,128)S(1)}, f32[512,256]{1,0:T(8,128)S(1)}, u32[]{:S(2)}, u32[]{:S(2)}) %collective-permute-start.3) | collective-permute-done | bytes 524320 | tf_op jit(solution)/shard_map/ppermute | solution.py:325
  29.0 1.9 %collective-permute-start.4 = (f32[512,256]{1,0:T(8,128)S(1)}, f32[512,256]{1,0:T(8,128)S(1)}, u32[]{:S(2)}, u32[]{:S(2)}) collective-permute-start(f32[512,256]{1,0:T(8,128)S(1)} %collective-permute-done.3.refs_5_.refs_14_), channel_id=1, source_target_pairs={{1,2},{5,6},{9,10},{13,14},{17,18},{21,22},{25,26},{29,30},{2,3},{... | collective-permute-start | bytes 1572872 | tf_op jit(solution)/shard_map/ppermute | solution.py:325
  31.7 1.4 collective-permute-start.14
  33.7 1.7 %broadcast_select_fusion.8 = f32[256,256]{1,0:T(8,128)} fusion(f32[256,256]{1,0:T(8,128)} %collective-permute-done.9, f32[256,256]{1,0:T(8,128)} %broadcast_select_fusion.7, pred[]{:T(512)S(6)} %and.95), kind=kLoop, calls=%fused_computation.18 | loop fusion | flops 65536 | bytes 786433 | tf_op jit(solution)/shard_map/jit(_where)/select_n | solution.py:358
  35.4 3.3 %collective-permute-start.10 = (f32[256,256]{1,0:T(8,128)}, f32[256,256]{1,0:T(8,128)}, u32[]{:S(2)}, u32[]{:S(2)}) collective-permute-start(f32[256,256]{1,0:T(8,128)} %broadcast_select_fusion.8), channel_id=1, source_target_pairs={{0,4},{1,5},{2,6},{3,7},{8,12},{9,13},{10,14},{11,15},{16,20},{17,... | collective-permute-start | bytes 786440 | tf_op jit(solution)/shard_map/ppermute | solution.py:325
  38.7 1.6 collective-permute-done.refs_1_.refs_10_
  40.2 1.9 %collective-permute-start.1 = (f32[512,256]{1,0:T(8,128)S(1)}, f32[512,256]{1,0:T(8,128)S(1)}, u32[]{:S(2)}, u32[]{:S(2)}) collective-permute-start(f32[512,256]{1,0:T(8,128)S(1)} %collective-permute-done.refs_1_.refs_10_), channel_id=1, source_target_pairs={{1,2},{5,6},{9,10},{13,14},{17,18},{21,22},{25,26},{29,30},{2,3},{... | collective-permute-start | bytes 1572872 | tf_op jit(solution)/shard_map/ppermute | solution.py:325
  42.1 9.3 %collective-permute-done.4.refs_6_.refs_15_ = f32[512,256]{1,0:T(8,128)S(1)} collective-permute-done((f32[512,256]{1,0:T(8,128)S(1)}, f32[512,256]{1,0:T(8,128)S(1)}, u32[]{:S(2)}, u32[]{:S(2)}) %collective-permute-start.4) | collective-permute-done | bytes 524320 | tf_op jit(solution)/shard_map/ppermute | solution.py:325
  51.5 2.1 %collective-permute-start.5 = (f32[512,256]{1,0:T(8,128)S(1)}, f32[512,256]{1,0:T(8,128)}, u32[]{:S(2)}, u32[]{:S(2)}) collective-permute-start(f32[512,256]{1,0:T(8,128)S(1)} %collective-permute-done.4.refs_6_.refs_15_), channel_id=1, source_target_pairs={{2,3},{6,7},{10,11},{14,15},{18,19},{22,23},{26,27},{30,31}} | collective-permute-start | bytes 1572872 | tf_op jit(solution)/shard_map/ppermute | solution.py:325
  57.7 5.0 %collective-permute-done.1.refs_2_.refs_11_ = f32[512,256]{1,0:T(8,128)S(1)} collective-permute-done((f32[512,256]{1,0:T(8,128)S(1)}, f32[512,256]{1,0:T(8,128)S(1)}, u32[]{:S(2)}, u32[]{:S(2)}) %collective-permute-start.1) | collective-permute-done | bytes 524320 | tf_op jit(solution)/shard_map/ppermute | solution.py:325
  62.6 1.3 collective-permute-start.2
  64.0 1.6 collective-permute-done.5.refs_7_
  66.8 1.3 collective-permute-start.23
  68.2 1.3 collective-permute-start.16
  69.5 1.3 collective-permute-start.19
  70.8 5.4 %collective-permute-done.2.refs_3_ = f32[512,256]{1,0:T(8,128)S(1)} collective-permute-done((f32[512,256]{1,0:T(8,128)S(1)}, f32[512,256]{1,0:T(8,128)S(1)}, u32[]{:S(2)}, u32[]{:S(2)}) %collective-permute-start.2) | collective-permute-done | bytes 524320 | tf_op jit(solution)/shard_map/ppermute | solution.py:325
  76.4 1.3 collective-permute-start.21
  77.7 1.3 collective-permute-start.17
  79.1 1.9 %collective-permute-start.31 = (f32[512,256]{1,0:T(8,128)S(1)}, f32[512,256]{1,0:T(8,128)S(1)}, u32[]{:S(2)}, u32[]{:S(2)}) collective-permute-start(f32[512,256]{1,0:T(8,128)S(1)} %broadcast_select_fusion.refs_6_), channel_id=1, source_target_pairs={{0,16},{16,0},{8,24},{24,8},{5,21},{21,5},{13,29},{29,13},{10,26},... | collective-permute-start | bytes 1572872 | tf_op jit(solution)/shard_map/ppermute | solution.py:325
  81.0 2.5 %collective-permute-done.19 = f32[512,256]{1,0:T(8,128)S(1)} collective-permute-done((f32[512,256]{1,0:T(8,128)S(1)}, f32[512,256]{1,0:T(8,128)S(1)}, u32[]{:S(2)}, u32[]{:S(2)}) %collective-permute-start.19) | collective-permute-done | bytes 524320 | tf_op jit(solution)/shard_map/ppermute | solution.py:325
  83.5 1.3 collective-permute-start.24
  84.9 4.2 %collective-permute-done.21 = f32[512,256]{1,0:T(8,128)S(1)} collective-permute-done((f32[512,256]{1,0:T(8,128)S(1)}, f32[512,256]{1,0:T(8,128)S(1)}, u32[]{:S(2)}, u32[]{:S(2)}) %collective-permute-start.21) | collective-permute-done | bytes 524320 | tf_op jit(solution)/shard_map/ppermute | solution.py:325
  89.1 1.9 %collective-permute-start.27 = (f32[512,256]{1,0:T(8,128)S(1)}, f32[512,256]{1,0:T(8,128)S(1)}, u32[]{:S(2)}, u32[]{:S(2)}) collective-permute-start(f32[512,256]{1,0:T(8,128)S(1)} %broadcast_select_fusion.2.refs_2_), channel_id=1, source_target_pairs={{0,16},{16,0},{8,24},{24,8},{5,21},{21,5},{13,29},{29,13},{10,26},... | collective-permute-start | bytes 1572872 | tf_op jit(solution)/shard_map/ppermute | solution.py:325
  91.1 3.6 %collective-permute-done.17 = f32[512,256]{1,0:T(8,128)S(1)} collective-permute-done((f32[512,256]{1,0:T(8,128)S(1)}, f32[512,256]{1,0:T(8,128)S(1)}, u32[]{:S(2)}, u32[]{:S(2)}) %collective-permute-start.17) | collective-permute-done | bytes 524320 | tf_op jit(solution)/shard_map/ppermute | solution.py:325
  94.8 1.3 collective-permute-start.20
  96.2 1.9 %collective-permute-start.29 = (f32[512,256]{1,0:T(8,128)S(1)}, f32[512,256]{1,0:T(8,128)S(1)}, u32[]{:S(2)}, u32[]{:S(2)}) collective-permute-start(f32[512,256]{1,0:T(8,128)S(1)} %broadcast_select_fusion.1.refs_4_), channel_id=1, source_target_pairs={{0,16},{16,0},{8,24},{24,8},{5,21},{21,5},{13,29},{29,13},{10,26},... | collective-permute-start | bytes 1572872 | tf_op jit(solution)/shard_map/ppermute | solution.py:325
  98.1 1.3 collective-permute-start.22
  99.5 3.9 %collective-permute-start.25 = (f32[512,256]{1,0:T(8,128)S(1)}, f32[512,256]{1,0:T(8,128)S(1)}, u32[]{:S(2)}, u32[]{:S(2)}) collective-permute-start(f32[512,256]{1,0:T(8,128)S(1)} %broadcast_select_fusion.3.refs_0_), channel_id=1, source_target_pairs={{0,16},{16,0},{8,24},{24,8},{5,21},{21,5},{13,29},{29,13},{10,26},... | collective-permute-start | bytes 1572872 | tf_op jit(solution)/shard_map/ppermute | solution.py:325
  103.4 8.6 %first_inverse.1.inverse.refs_16_ = f32[256,256]{1,0:T(8,128)S(1)} custom-call(f32[256,256]{1,0:T(8,128)S(1)} %broadcast_select_fusion.9.tile), custom_call_target="tpu_custom_call" | custom-call | flops 8589934592 | bytes 1048576 | tf_op jit(solution)/shard_map/first_inverse/pallas_call | solution.py:112
  112.1 1.3 collective-permute-start.18
  113.4 1.3 collective-permute-start.32
  114.8 1.3 collective-permute-start.28
  116.1 1.3 collective-permute-start.30
  117.5 2.1 %collective-permute-start.26 = (f32[512,256]{1,0:T(8,128)S(1)}, f32[512,256]{1,0:T(8,128)}, u32[]{:S(2)}, u32[]{:S(2)}) collective-permute-start(f32[512,256]{1,0:T(8,128)S(1)} %collective-permute-done.25.refs_8_), channel_id=1, source_target_pairs={{0,4},{16,20},{8,12},{24,28},{5,1},{21,17},{13,9},{29,25},{10,14},... | collective-permute-start | bytes 1572872 | tf_op jit(solution)/shard_map/ppermute | solution.py:325
  119.5 11.7 %second_inverse.1 = (f32[256,256]{1,0:T(8,128)S(1)}, f32[256,256]{1,0:T(8,128)S(1)}) custom-call(s32[1]{0:T(128)} %bitcast.6.rank, f32[512,256]{1,0:T(8,128)S(1)} %broadcast_select_fusion.6.head, f32[256,256]{1,0:T(8,128)S(1)} %first_inverse.1.inverse.refs_16_), custom_call_target="tpu_custom_call" | custom-call | flops 8589934592 | bytes 1048576 | tf_op jit(solution)/shard_map/second_inverse/pallas_call | solution.py:140
  131.3 4.4 %row_panels.1 = (bf16[4,256,512]{2,1,0:T(8,128)(2,1)}, bf16[4,256,512]{2,1,0:T(8,128)(2,1)}) custom-call(s32[5]{0:T(128)S(1)} %broadcast_in_dim.37.choice, s32[1,8]{1,0:T(1,128)S(1)} %reshape.115.offsets, s32[1,8]{1,0:T(1,128)S(1)} %reshape.116.ranks, f32[512,256]{1,0:T(8,128)S(1)} %get-tuple-element.13.refs_0_.refs_9_, ...), custom_call_target="tpu_custom_call" | custom-call | flops 2147483648 | bytes 4194304 | tf_op jit(solution)/shard_map/row_panels/pallas_call | solution.py:247
  137.0 8.3 %col_panels.1 = (bf16[8,256,512]{2,1,0:T(8,128)(2,1)}, bf16[8,256,512]{2,1,0:T(8,128)(2,1)}) custom-call(s32[10]{0:T(128)S(1)} %pad_add_fusion.3.choice, s32[2,8]{1,0:T(2,128)S(1)} %pad_add_fusion.offsets, s32[2,8]{1,0:T(2,128)S(1)} %pad_add_fusion.1.ranks, f32[512,256]{1,0:T(8,128)S(1)} %broadcast_select_fusion.3.refs_0_, ...), custom_call_target="tpu_custom_call" | custom-call | flops 4294967296 | bytes 8388608 | tf_op jit(solution)/shard_map/col_panels/pallas_call | solution.py:247
  145.3 21.6 %schur.1 = f32[4,8,256,256]{3,2,1,0:T(8,128)} custom-call(s32[4]{0:T(128)S(1)} %pad_add_fusion.2.place, s32[4,8]{1,0:T(4,128)S(1)} %select_bitcast_fusion.ranks, bf16[4,8,256,128]{3,2,1,0:T(8,128)(2,1)S(1)} %copy-done.1, bf16[4,8,256,128]{3,2,1,0:T(8,128)(2,1)} %right.3, bf16[4,256,512]{2,1,0:T(8,128)(2,1)S(1)} %copy-done.3, ...), custom_call_target="tpu_custom_call" | custom-call | flops 8589934592 | bytes 16777216 | tf_op jit(solution)/shard_map/schur/pallas_call | solution.py:298
  (99 shorter events, 16.0 us)
Async XLA Ops:
  1.3 1.6 copy-start
  2.9 1.6 copy-start.2
  4.5 10.6 %copy-start.6 = (s32[32,32]{1,0:T(8,128)S(1)}, s32[32,32]{1,0:T(8,128)}, u32[]{:S(2)}) copy-start(s32[32,32]{1,0:T(8,128)} %param.7) | copy-start | bytes 12292
  5.9 15.3 %collective-permute-start.13 = (f32[256,256]{1,0:T(8,128)S(1)}, f32[256,256]{1,0:T(8,128)S(1)}, u32[]{:S(2)}, u32[]{:S(2)}) collective-permute-start(f32[256,256]{1,0:T(8,128)S(1)} %pad_maximum_fusion.1), channel_id=1, source_target_pairs={{4,7}} | collective-permute-start | bytes 786440 | tf_op jit(solution)/shard_map/ppermute | solution.py:325
  6.5 16.0 %collective-permute-start.12 = (f32[256,256]{1,0:T(8,128)S(1)}, f32[256,256]{1,0:T(8,128)S(1)}, u32[]{:S(2)}, u32[]{:S(2)}) collective-permute-start(f32[256,256]{1,0:T(8,128)S(1)} %pad_maximum_fusion.1), channel_id=1, source_target_pairs={{4,6}} | collective-permute-start | bytes 786440 | tf_op jit(solution)/shard_map/ppermute | solution.py:325
  7.2 17.3 %collective-permute-start.11 = (f32[256,256]{1,0:T(8,128)S(1)}, f32[256,256]{1,0:T(8,128)}, u32[]{:S(2)}, u32[]{:S(2)}) collective-permute-start(f32[256,256]{1,0:T(8,128)S(1)} %pad_maximum_fusion.1), channel_id=1, source_target_pairs={{4,5}} | collective-permute-start | bytes 786440 | tf_op jit(solution)/shard_map/ppermute | solution.py:325
  8.6 20.4 %collective-permute-start.3 = (f32[512,256]{1,0:T(8,128)S(1)}, f32[512,256]{1,0:T(8,128)S(1)}, u32[]{:S(2)}, u32[]{:S(2)}) collective-permute-start(f32[512,256]{1,0:T(8,128)S(1)} %get-tuple-element.14.refs_4_.refs_13_), channel_id=1, source_target_pairs={{0,1},{4,5},{8,9},{12,13},{16,17},{20,21},{24,25},{28,29},{1,2},{5... | collective-permute-start | bytes 1572872 | tf_op jit(solution)/shard_map/ppermute | solution.py:325
  10.8 22.8 %copy-start.5 = (f32[256,256]{1,0:T(8,128)}, f32[256,256]{1,0:T(8,128)S(1)}, u32[]{:S(2)}) copy-start(f32[256,256]{1,0:T(8,128)S(1)} %slice_bitcast_fusion) | copy-start | bytes 786436
  10.9 7.3 %collective-permute-start.8 = (f32[256,256]{1,0:T(8,128)S(1)}, f32[256,256]{1,0:T(8,128)}, u32[]{:S(2)}, u32[]{:S(2)}) collective-permute-start(f32[256,256]{1,0:T(8,128)S(1)} %slice_bitcast_fusion), channel_id=1, source_target_pairs={{0,8},{1,9},{2,10},{3,11}} | collective-permute-start | bytes 786440 | tf_op jit(solution)/shard_map/ppermute | solution.py:325
  18.1 22.1 %collective-permute-start = (f32[512,256]{1,0:T(8,128)S(1)}, f32[512,256]{1,0:T(8,128)S(1)}, u32[]{:S(2)}, u32[]{:S(2)}) collective-permute-start(f32[512,256]{1,0:T(8,128)S(1)} %get-tuple-element.13.refs_0_.refs_9_), channel_id=1, source_target_pairs={{0,1},{4,5},{8,9},{12,13},{16,17},{20,21},{24,25},{28,29},{1,2},{5... | collective-permute-start | bytes 1572872 | tf_op jit(solution)/shard_map/ppermute | solution.py:325
  21.1 42.8 %collective-permute-start.7 = (f32[512,256]{1,0:T(8,128)S(1)}, f32[512,256]{1,0:T(8,128)}, u32[]{:S(2)}, u32[]{:S(2)}) collective-permute-start(f32[512,256]{1,0:T(8,128)S(1)} %get-tuple-element.14.refs_4_.refs_13_), channel_id=1, source_target_pairs={{1,0},{5,4},{9,8},{13,12},{17,16},{21,20},{25,24},{29,28}} | collective-permute-start | bytes 1572872 | tf_op jit(solution)/shard_map/ppermute | solution.py:325
  22.6 11.1 %collective-permute-start.9 = (f32[256,256]{1,0:T(8,128)}, f32[256,256]{1,0:T(8,128)}, u32[]{:S(2)}, u32[]{:S(2)}) collective-permute-start(f32[256,256]{1,0:T(8,128)} %broadcast_select_fusion.7), channel_id=1, source_target_pairs={{0,16},{1,17},{2,18},{3,19},{8,24},{9,25},{10,26},{11,27}} | collective-permute-start | bytes 786440 | tf_op jit(solution)/shard_map/ppermute | solution.py:325
  29.0 22.5 %collective-permute-start.4 = (f32[512,256]{1,0:T(8,128)S(1)}, f32[512,256]{1,0:T(8,128)S(1)}, u32[]{:S(2)}, u32[]{:S(2)}) collective-permute-start(f32[512,256]{1,0:T(8,128)S(1)} %collective-permute-done.3.refs_5_.refs_14_), channel_id=1, source_target_pairs={{1,2},{5,6},{9,10},{13,14},{17,18},{21,22},{25,26},{29,30},{2,3},{... | collective-permute-start | bytes 1572872 | tf_op jit(solution)/shard_map/ppermute | solution.py:325
  31.7 22.5 %collective-permute-start.14 = (f32[512,256]{1,0:T(8,128)}, f32[512,256]{1,0:T(8,128)}, u32[]{:S(2)}, u32[]{:S(2)}) collective-permute-start(f32[512,256]{1,0:T(8,128)} %pad_maximum_fusion), channel_id=1, source_target_pairs={{4,12},{5,13},{6,14},{7,15}} | collective-permute-start | bytes 1572872 | tf_op jit(solution)/shard_map/ppermute | solution.py:325
  35.4 20.6 %collective-permute-start.10 = (f32[256,256]{1,0:T(8,128)}, f32[256,256]{1,0:T(8,128)}, u32[]{:S(2)}, u32[]{:S(2)}) collective-permute-start(f32[256,256]{1,0:T(8,128)} %broadcast_select_fusion.8), channel_id=1, source_target_pairs={{0,4},{1,5},{2,6},{3,7},{8,12},{9,13},{10,14},{11,15},{16,20},{17,... | collective-permute-start | bytes 786440 | tf_op jit(solution)/shard_map/ppermute | solution.py:325
  40.2 22.4 %collective-permute-start.1 = (f32[512,256]{1,0:T(8,128)S(1)}, f32[512,256]{1,0:T(8,128)S(1)}, u32[]{:S(2)}, u32[]{:S(2)}) collective-permute-start(f32[512,256]{1,0:T(8,128)S(1)} %collective-permute-done.refs_1_.refs_10_), channel_id=1, source_target_pairs={{1,2},{5,6},{9,10},{13,14},{17,18},{21,22},{25,26},{29,30},{2,3},{... | collective-permute-start | bytes 1572872 | tf_op jit(solution)/shard_map/ppermute | solution.py:325
  51.5 14.2 %collective-permute-start.5 = (f32[512,256]{1,0:T(8,128)S(1)}, f32[512,256]{1,0:T(8,128)}, u32[]{:S(2)}, u32[]{:S(2)}) collective-permute-start(f32[512,256]{1,0:T(8,128)S(1)} %collective-permute-done.4.refs_6_.refs_15_), channel_id=1, source_target_pairs={{2,3},{6,7},{10,11},{14,15},{18,19},{22,23},{26,27},{30,31}} | collective-permute-start | bytes 1572872 | tf_op jit(solution)/shard_map/ppermute | solution.py:325
  54.2 16.6 %collective-permute-start.6 = (f32[512,256]{1,0:T(8,128)S(1)}, f32[512,256]{1,0:T(8,128)S(1)}, u32[]{:S(2)}, u32[]{:S(2)}) collective-permute-start(f32[512,256]{1,0:T(8,128)S(1)} %get-tuple-element.13.refs_0_.refs_9_), channel_id=1, source_target_pairs={{1,0},{5,4},{9,8},{13,12},{17,16},{21,20},{25,24},{29,28}} | collective-permute-start | bytes 1572872 | tf_op jit(solution)/shard_map/ppermute | solution.py:325
  56.0 12.2 %collective-permute-start.15 = (f32[512,256]{1,0:T(8,128)S(1)}, f32[512,256]{1,0:T(8,128)S(1)}, u32[]{:S(2)}, u32[]{:S(2)}) collective-permute-start(f32[512,256]{1,0:T(8,128)S(1)} %broadcast_select_fusion.4), channel_id=1, source_target_pairs={{4,20},{5,21},{6,22},{7,23},{12,28},{13,29},{14,30},{15,31}} | collective-permute-start | bytes 1572872 | tf_op jit(solution)/shard_map/ppermute | solution.py:325
  62.6 13.6 %collective-permute-start.2 = (f32[512,256]{1,0:T(8,128)S(1)}, f32[512,256]{1,0:T(8,128)S(1)}, u32[]{:S(2)}, u32[]{:S(2)}) collective-permute-start(f32[512,256]{1,0:T(8,128)S(1)} %collective-permute-done.1.refs_2_.refs_11_), channel_id=1, source_target_pairs={{2,3},{6,7},{10,11},{14,15},{18,19},{22,23},{26,27},{30,31}} | collective-permute-start | bytes 1572872 | tf_op jit(solution)/shard_map/ppermute | solution.py:325
  66.8 12.2 %collective-permute-start.23 = (f32[512,256]{1,0:T(8,128)S(1)}, f32[512,256]{1,0:T(8,128)S(1)}, u32[]{:S(2)}, u32[]{:S(2)}) collective-permute-start(f32[512,256]{1,0:T(8,128)S(1)} %get-tuple-element.26), channel_id=1, source_target_pairs={{0,8},{16,24},{5,13},{21,29},{10,2},{26,18},{15,7},{31,23}} | collective-permute-start | bytes 1572872 | tf_op jit(solution)/shard_map/ppermute | solution.py:325
  68.2 27.9 %collective-permute-start.16 = (f32[512,256]{1,0:T(8,128)S(1)}, f32[512,256]{1,0:T(8,128)S(1)}, u32[]{:S(2)}, u32[]{:S(2)}) collective-permute-start(f32[512,256]{1,0:T(8,128)S(1)} %broadcast_select_fusion.5), channel_id=1, source_target_pairs={{4,0},{5,1},{6,2},{7,3},{12,8},{13,9},{14,10},{15,11},{20,16},{21,... | collective-permute-start | bytes 1572872 | tf_op jit(solution)/shard_map/ppermute | solution.py:325
  69.5 14.0 %collective-permute-start.19 = (f32[512,256]{1,0:T(8,128)S(1)}, f32[512,256]{1,0:T(8,128)S(1)}, u32[]{:S(2)}, u32[]{:S(2)}) collective-permute-start(f32[512,256]{1,0:T(8,128)S(1)} %get-tuple-element.27), channel_id=1, source_target_pairs={{0,8},{16,24},{5,13},{21,29},{10,2},{26,18},{15,7},{31,23}} | collective-permute-start | bytes 1572872 | tf_op jit(solution)/shard_map/ppermute | solution.py:325
  76.4 12.7 %collective-permute-start.21 = (f32[512,256]{1,0:T(8,128)S(1)}, f32[512,256]{1,0:T(8,128)S(1)}, u32[]{:S(2)}, u32[]{:S(2)}) collective-permute-start(f32[512,256]{1,0:T(8,128)S(1)} %get-tuple-element.28), channel_id=1, source_target_pairs={{0,8},{16,24},{5,13},{21,29},{10,2},{26,18},{15,7},{31,23}} | collective-permute-start | bytes 1572872 | tf_op jit(solution)/shard_map/ppermute | solution.py:325
  77.7 17.0 %collective-permute-start.17 = (f32[512,256]{1,0:T(8,128)S(1)}, f32[512,256]{1,0:T(8,128)S(1)}, u32[]{:S(2)}, u32[]{:S(2)}) collective-permute-start(f32[512,256]{1,0:T(8,128)S(1)} %get-tuple-element.29), channel_id=1, source_target_pairs={{0,8},{16,24},{5,13},{21,29},{10,2},{26,18},{15,7},{31,23}} | collective-permute-start | bytes 1572872 | tf_op jit(solution)/shard_map/ppermute | solution.py:325
  79.1 19.0 %collective-permute-start.31 = (f32[512,256]{1,0:T(8,128)S(1)}, f32[512,256]{1,0:T(8,128)S(1)}, u32[]{:S(2)}, u32[]{:S(2)}) collective-permute-start(f32[512,256]{1,0:T(8,128)S(1)} %broadcast_select_fusion.refs_6_), channel_id=1, source_target_pairs={{0,16},{16,0},{8,24},{24,8},{5,21},{21,5},{13,29},{29,13},{10,26},... | collective-permute-start | bytes 1572872 | tf_op jit(solution)/shard_map/ppermute | solution.py:325
  83.5 15.9 %collective-permute-start.24 = (f32[512,256]{1,0:T(8,128)S(1)}, f32[512,256]{1,0:T(8,128)S(1)}, u32[]{:S(2)}, u32[]{:S(2)}) collective-permute-start(f32[512,256]{1,0:T(8,128)S(1)} %broadcast_select_fusion.refs_6_), channel_id=1, source_target_pairs={{0,4},{16,20},{8,12},{24,28},{5,1},{21,17},{13,9},{29,25},{10,14},... | collective-permute-start | bytes 1572872 | tf_op jit(solution)/shard_map/ppermute | solution.py:325
  89.1 22.9 %collective-permute-start.27 = (f32[512,256]{1,0:T(8,128)S(1)}, f32[512,256]{1,0:T(8,128)S(1)}, u32[]{:S(2)}, u32[]{:S(2)}) collective-permute-start(f32[512,256]{1,0:T(8,128)S(1)} %broadcast_select_fusion.2.refs_2_), channel_id=1, source_target_pairs={{0,16},{16,0},{8,24},{24,8},{5,21},{21,5},{13,29},{29,13},{10,26},... | collective-permute-start | bytes 1572872 | tf_op jit(solution)/shard_map/ppermute | solution.py:325
  94.8 18.6 %collective-permute-start.20 = (f32[512,256]{1,0:T(8,128)S(1)}, f32[512,256]{1,0:T(8,128)S(1)}, u32[]{:S(2)}, u32[]{:S(2)}) collective-permute-start(f32[512,256]{1,0:T(8,128)S(1)} %broadcast_select_fusion.2.refs_2_), channel_id=1, source_target_pairs={{0,4},{16,20},{8,12},{24,28},{5,1},{21,17},{13,9},{29,25},{10,14},... | collective-permute-start | bytes 1572872 | tf_op jit(solution)/shard_map/ppermute | solution.py:325
  96.2 18.6 %collective-permute-start.29 = (f32[512,256]{1,0:T(8,128)S(1)}, f32[512,256]{1,0:T(8,128)S(1)}, u32[]{:S(2)}, u32[]{:S(2)}) collective-permute-start(f32[512,256]{1,0:T(8,128)S(1)} %broadcast_select_fusion.1.refs_4_), channel_id=1, source_target_pairs={{0,16},{16,0},{8,24},{24,8},{5,21},{21,5},{13,29},{29,13},{10,26},... | collective-permute-start | bytes 1572872 | tf_op jit(solution)/shard_map/ppermute | solution.py:325
  98.1 15.3 %copy-start.7 = (f32[512,256]{1,0:T(8,128)}, f32[512,256]{1,0:T(8,128)S(1)}, u32[]{:S(2)}) copy-start(f32[512,256]{1,0:T(8,128)S(1)} %collective-permute-done.31.refs_14_) | copy-start | bytes 1572868
  98.1 18.0 %collective-permute-start.22 = (f32[512,256]{1,0:T(8,128)S(1)}, f32[512,256]{1,0:T(8,128)S(1)}, u32[]{:S(2)}, u32[]{:S(2)}) collective-permute-start(f32[512,256]{1,0:T(8,128)S(1)} %broadcast_select_fusion.1.refs_4_), channel_id=1, source_target_pairs={{0,4},{16,20},{8,12},{24,28},{5,1},{21,17},{13,9},{29,25},{10,14},... | collective-permute-start | bytes 1572872 | tf_op jit(solution)/shard_map/ppermute | solution.py:325
  99.5 18.0 %collective-permute-start.25 = (f32[512,256]{1,0:T(8,128)S(1)}, f32[512,256]{1,0:T(8,128)S(1)}, u32[]{:S(2)}, u32[]{:S(2)}) collective-permute-start(f32[512,256]{1,0:T(8,128)S(1)} %broadcast_select_fusion.3.refs_0_), channel_id=1, source_target_pairs={{0,16},{16,0},{8,24},{24,8},{5,21},{21,5},{13,29},{29,13},{10,26},... | collective-permute-start | bytes 1572872 | tf_op jit(solution)/shard_map/ppermute | solution.py:325
  112.1 19.2 %copy-start.8 = (f32[512,256]{1,0:T(8,128)}, f32[512,256]{1,0:T(8,128)S(1)}, u32[]{:S(2)}) copy-start(f32[512,256]{1,0:T(8,128)S(1)} %collective-permute-done.27.refs_10_) | copy-start | bytes 1572868
  112.1 23.6 %collective-permute-start.18 = (f32[512,256]{1,0:T(8,128)S(1)}, f32[512,256]{1,0:T(8,128)S(1)}, u32[]{:S(2)}, u32[]{:S(2)}) collective-permute-start(f32[512,256]{1,0:T(8,128)S(1)} %broadcast_select_fusion.3.refs_0_), channel_id=1, source_target_pairs={{0,4},{16,20},{8,12},{24,28},{5,1},{21,17},{13,9},{29,25},{10,14},... | collective-permute-start | bytes 1572872 | tf_op jit(solution)/shard_map/ppermute | solution.py:325
  113.4 22.3 %collective-permute-start.32 = (f32[512,256]{1,0:T(8,128)S(1)}, f32[512,256]{1,0:T(8,128)S(1)}, u32[]{:S(2)}, u32[]{:S(2)}) collective-permute-start(f32[512,256]{1,0:T(8,128)S(1)} %collective-permute-done.31.refs_14_), channel_id=1, source_target_pairs={{0,4},{16,20},{8,12},{24,28},{5,1},{21,17},{13,9},{29,25},{10,14},... | collective-permute-start | bytes 1572872 | tf_op jit(solution)/shard_map/ppermute | solution.py:325
  114.8 16.5 %copy-start.9 = (f32[512,256]{1,0:T(8,128)}, f32[512,256]{1,0:T(8,128)S(1)}, u32[]{:S(2)}) copy-start(f32[512,256]{1,0:T(8,128)S(1)} %collective-permute-done.29.refs_12_) | copy-start | bytes 1572868
  114.8 21.0 %collective-permute-start.28 = (f32[512,256]{1,0:T(8,128)S(1)}, f32[512,256]{1,0:T(8,128)S(1)}, u32[]{:S(2)}, u32[]{:S(2)}) collective-permute-start(f32[512,256]{1,0:T(8,128)S(1)} %collective-permute-done.27.refs_10_), channel_id=1, source_target_pairs={{0,4},{16,20},{8,12},{24,28},{5,1},{21,17},{13,9},{29,25},{10,14},... | collective-permute-start | bytes 1572872 | tf_op jit(solution)/shard_map/ppermute | solution.py:325
  116.1 19.6 %collective-permute-start.30 = (f32[512,256]{1,0:T(8,128)S(1)}, f32[512,256]{1,0:T(8,128)S(1)}, u32[]{:S(2)}, u32[]{:S(2)}) collective-permute-start(f32[512,256]{1,0:T(8,128)S(1)} %collective-permute-done.29.refs_12_), channel_id=1, source_target_pairs={{0,4},{16,20},{8,12},{24,28},{5,1},{21,17},{13,9},{29,25},{10,14},... | collective-permute-start | bytes 1572872 | tf_op jit(solution)/shard_map/ppermute | solution.py:325
  117.5 18.3 %collective-permute-start.26 = (f32[512,256]{1,0:T(8,128)S(1)}, f32[512,256]{1,0:T(8,128)}, u32[]{:S(2)}, u32[]{:S(2)}) collective-permute-start(f32[512,256]{1,0:T(8,128)S(1)} %collective-permute-done.25.refs_8_), channel_id=1, source_target_pairs={{0,4},{16,20},{8,12},{24,28},{5,1},{21,17},{13,9},{29,25},{10,14},... | collective-permute-start | bytes 1572872 | tf_op jit(solution)/shard_map/ppermute | solution.py:325
  135.7 9.6 %copy-start.1 = (bf16[4,8,256,128]{3,2,1,0:T(8,128)(2,1)S(1)}, bf16[4,8,256,128]{3,2,1,0:T(8,128)(2,1)}, u32[]{:S(2)}) copy-start(bf16[4,8,256,128]{3,2,1,0:T(8,128)(2,1)} %left.3) | copy-start | bytes 6291460
  135.7 9.6 %copy-start.3 = (bf16[4,256,512]{2,1,0:T(8,128)(2,1)S(1)}, bf16[4,256,512]{2,1,0:T(8,128)(2,1)}, u32[]{:S(2)}) copy-start(bf16[4,256,512]{2,1,0:T(8,128)(2,1)} %get-tuple-element.17.row_high) | copy-start | bytes 3145732
  135.7 9.6 %copy-start.4 = (bf16[4,256,512]{2,1,0:T(8,128)(2,1)S(1)}, bf16[4,256,512]{2,1,0:T(8,128)(2,1)}, u32[]{:S(2)}) copy-start(bf16[4,256,512]{2,1,0:T(8,128)(2,1)} %get-tuple-element.18.row_low) | copy-start | bytes 3145732
  135.7 0.8 copy-start.10
  135.7 1.0 copy-start.11
  135.8 1.2 copy-start.12
